TPU v7x, 32 devices: a whole 2x2x4 slice. The times are simulated.
32 devices in a mesh: fsdp: 8 (over y, x, core), rep: 4 (over z).
Axes of the slice: x: 2, y: 2, z: 4, core: 2. Of those that a mesh axis runs over, the one named last changes fastest.
Arguments:
- tokens: bfloat16 [12288, 1600], P(('fsdp', 'rep')), may hold values from -41 to 41
- norm_gain: float32 [1600], replicated, may hold values from 0.1 to 1.9
- up_weight: bfloat16 [6400, 1600], P('fsdp'), may hold values from -0.15625 to 0.15625
- up_bias: bfloat16 [6400], P('fsdp'), may hold values from -3 to 3
- keep_mask: int32 [128], P(('fsdp', 'rep')), may hold values 0 or 1
- cotangent: bfloat16 [12288, 6400], P(('fsdp', 'rep')), may hold values from -6 to 6
Outputs:
- hidden: bfloat16 [12288, 6400], P(('fsdp', 'rep'))
- grad_in: bfloat16 [12288, 1600], P(('fsdp', 'rep'))
- grad_weight: float32 [6400, 1600], P('fsdp')
- grad_bias: float32 [6400], P('fsdp')
- grad_gain: float32 [1600], replicated
All inputs are finite; a program needn't handle non-finite values. No bound on the sum of `keep_mask` on one device may be relied on, other than what follows from the above.
Results may differ from a plain program's by a relative error of at most 0.02.
Values may be sent and summed in bfloat16 or wider, within the bound.
No kernel may reach another device: no remote copies, remote signals or barrier semaphores. Data moves between devices by JAX's collectives and lax.ppermute only.
A program may use at most 192 MiB of HBM per device.

v0:
```python
import functools
import math

import jax
import jax.numpy as jnp
from jax import lax
from jax.experimental import pallas as pl
from jax.experimental.pallas import tpu as pltpu
from jax.sharding import PartitionSpec as P

CHUNKS = (192, 192, 160, 160, 96)
ORDER = (
    "Oa r0 W0 r1 ",
    "W1 B0 B1 W2 ",
    "B2 R0 R1 Ob ",
    "S0 S1 T0 W3 ",
    "B3 W4 V0 T1 ",
    "R2 B4 R3 U0 ",
    "G S2 V1 R4 ",
    "T2 ga S3 U1 ",
    "gb V2 gd T3 ",
    "S4 U2 T4 V3 ",
    "K V4 H J ",
    "U3 U4 ",
)


def normalize(tokens, norm_gain):
    values = tokens.astype(jnp.float32)
    mean_sq = jnp.mean(values * values, axis=1, keepdims=True)
    inv_rms = lax.rsqrt(mean_sq + 1e-06)
    x_hat = values * inv_rms
    return (x_hat, inv_rms, (x_hat * norm_gain[None, :]).astype(jnp.bfloat16))


def activate(preact):
    cdf = 0.5 * (1.0 + jax.scipy.special.erf(preact * 0.7071067811865476))
    density = jnp.exp(-0.5 * preact * preact) * 0.3989422804014327
    return (preact * cdf, cdf + preact * density)


def row_scales(keep_mask, total_rows):
    per_sample = keep_mask.astype(jnp.float32) * (4.0 / 3.0)
    return jnp.repeat(per_sample, total_rows // keep_mask.shape[0])


def contract_last(left, right):
    return lax.dot_general(
        left, right, (((1,), (1,)), ((), ())), preferred_element_type=jnp.float32
    )


def swap(value, bit):
    return lax.ppermute(value, "fsdp", [(i, i ^ bit) for i in range(8)])


def swap_core(value):
    return swap(value, 1)


def swap_x(value):
    return swap(value, 2)


def swap_y(value):
    return swap(value, 4)


LANES = 128


def work_body(sizes, spots, width, first, *refs):
    m = len(sizes)
    place, normed, flipped, scale = refs[:4]
    piece_hbm = refs[4 : 4 + m]
    outs = refs[4 + m + 3 + (not first) :]
    former = None if first else refs[4 + m + 3]
    states, acc, grad_hbm = outs[:2], outs[3], outs[4 : 4 + m]
    pre, cot, hid, piece_v, low_v, grad_v, in_sem, cot_sem, out_sem = outs[4 + m :]
    rows2 = normed.shape[0]
    rows = rows2 // 2
    depth = normed.shape[1]
    begin = [sum(sizes[:j]) for j in range(m)]

    def near(j):
        return pl.ds(begin[j], sizes[j])

    def spot(j):
        start, side = spots[j]
        return pl.ds(pl.multiple_of(start + width * (place[0] ^ side), 16), sizes[j])

    copy = pltpu.make_async_copy
    piece_in = [copy(piece_hbm[j], piece_v.at[near(j)], in_sem.at[j]) for j in range(m)]
    cot_in = [
        copy(states[i].at[spot(j)], cot.at[near(j), pl.ds(i * rows, rows)], cot_sem.at[2 * j + i])
        for j in range(m)
        for i in range(2)
    ]
    hid_out = [
        copy(hid.at[near(j), pl.ds(i * rows, rows)], states[i].at[spot(j)], out_sem.at[3 * j + i])
        for j in range(m)
        for i in range(2)
    ]
    grad_out = [copy(grad_v.at[near(j)], grad_hbm[j], out_sem.at[3 * j + 2]) for j in range(m)]

    for j in range(m):
        piece_in[j].start()
        for one in cot_in[2 * j : 2 * j + 2]:
            one.start()
    for j in range(m):
        size = sizes[j]
        piece_in[j].wait()
        pre[:size, :] = jnp.dot(piece_v[near(j), :], flipped[...], preferred_element_type=jnp.float32)
        for one in cot_in[2 * j : 2 * j + 2]:
            one.wait()

        @pl.loop(0, size // 16)
        def _(strip):
            here = pl.ds(pl.multiple_of(strip * 16, 16), 16)
            there = pl.ds(pl.multiple_of(begin[j] + strip * 16, 16), 16)
            for col in range(0, rows2, 2 * LANES):
                cols = pl.ds(col, 2 * LANES)
                gelu_out, slopes = activate(pre[here, cols])
                factor = scale[:, cols]
                hid[there, cols] = (gelu_out * factor).astype(jnp.bfloat16)
                grad = cot[there, cols].astype(jnp.float32) * factor * slopes
                low_v[there, cols] = grad.astype(jnp.bfloat16)

        for one in hid_out[2 * j : 2 * j + 2]:
            one.start()
        for col in range(0, depth, 4 * LANES):
            cols = pl.ds(col, min(4 * LANES, depth - col))
            grad_v[near(j), cols] = jnp.dot(
                low_v[near(j), :], normed[:, cols], preferred_element_type=jnp.float32
            ).astype(jnp.bfloat16)
        grad_out[j].start()
    turned = low_v[...].T
    for col in range(0, depth, 4 * LANES):
        cols = pl.ds(col, min(4 * LANES, depth - col))
        part = jnp.dot(turned, piece_v[:, cols], preferred_element_type=jnp.float32)
        acc[:, cols] = part if first else former[:, cols] + part
    for one in hid_out + grad_out:
        one.wait()


def call(body, operands, outs, aliases, scratch=(), limit=16):
    spec = {
        "hbm": pl.BlockSpec(memory_space=pltpu.HBM),
        "vmem": pl.BlockSpec(memory_space=pltpu.VMEM),
        "smem": pl.BlockSpec(memory_space=pltpu.SMEM),
    }
    return pl.pallas_call(
        body,
        out_shape=[jax.ShapeDtypeStruct(shape, dtype) for _, shape, dtype in outs],
        in_specs=[spec[space] for space, _ in operands],
        out_specs=[spec[space] for space, _, _ in outs],
        scratch_shapes=list(scratch),
        input_output_aliases=aliases,
        compiler_params=pltpu.CompilerParams(vmem_limit_bytes=limit * 1024 * 1024),
        cost_estimate=pl.CostEstimate(flops=0, bytes_accessed=0, transcendentals=0),
    )(*[value for _, value in operands])


def work(pieces, spots, width, place, normed, flipped, scale, states, token, acc):
    sizes = [piece.shape[0] for piece in pieces]
    m, total = len(sizes), sum(sizes)
    rows2, depth = normed.shape
    low = jnp.bfloat16
    first = acc is None
    results = call(
        functools.partial(work_body, sizes, spots, width, first),
        [("smem", place), ("vmem", normed), ("vmem", flipped), ("vmem", scale)]
        + [("hbm", piece) for piece in pieces]
        + [("hbm", states[0]), ("hbm", states[1]), ("hbm", token)]
        + ([] if first else [("vmem", acc)]),
        [("hbm", states[0].shape, low), ("hbm", states[1].shape, low)]
        + [("hbm", token.shape, token.dtype), ("vmem", (rows2, depth), jnp.float32)]
        + [("hbm", (size, depth), low) for size in sizes],
        {4 + m: 0, 5 + m: 1, 6 + m: 2} | ({} if first else {7 + m: 3}),
        [
            pltpu.VMEM((max(sizes), rows2), jnp.float32),
            pltpu.VMEM((total, rows2), low),
            pltpu.VMEM((total, rows2), low),
            pltpu.VMEM((total, depth), low),
            pltpu.VMEM((total, rows2), low),
            pltpu.VMEM((total, depth), low),
            pltpu.SemaphoreType.DMA((m,)),
            pltpu.SemaphoreType.DMA((2 * m,)),
            pltpu.SemaphoreType.DMA((3 * m,)),
        ],
        limit=26,
    )
    return results[:2], results[2], results[3], results[4:]


def tie(token, *done):
    return call(
        lambda *refs: None,
        [("hbm", value) for value in done] + [("hbm", token)],
        [("hbm", token.shape, token.dtype)],
        {len(done): 0},
        limit=4,
    )[0]


def repeat_body(value, token, token_out, out, sem):
    move = pltpu.make_async_copy(value, out, sem.at[0])
    move.start()
    move.wait()


def repeat(value, token):
    results = call(
        repeat_body,
        [("hbm", value), ("hbm", token)],
        [("hbm", token.shape, token.dtype), ("hbm", value.shape, value.dtype)],
        {1: 0},
        [pltpu.SemaphoreType.DMA((1,))],
        limit=4,
    )
    return results[1], results[0]


def total_body(count, halves, extra, *refs):
    place, terms = refs[0], refs[1 : 1 + count]
    values, result, sem = refs[-3:]
    outs = refs[-5:-3] if halves else refs[-4:-3]
    size, depth = terms[0].shape
    moves = [pltpu.make_async_copy(terms[i], values.at[i], sem.at[i]) for i in range(count)]
    for one in moves:
        one.start()
    for one in moves:
        one.wait()

    @pl.loop(0, size // 16)
    def _(strip):
        here = pl.ds(pl.multiple_of(strip * 16, 16), 16)
        total = values[0, here, :].astype(jnp.float32)
        for i in range(1, count):
            total = total + values[i, here, :].astype(jnp.float32)
        result[here, :] = total.astype(result.dtype)
        if extra:
            tail = pl.ds(depth - LANES, LANES)
            result[here, tail] = (total[:, depth - LANES :] + refs[1 + count][here, :]).astype(result.dtype)

    if halves:
        half = size // 2
        back = [
            pltpu.make_async_copy(
                result.at[pl.ds(pl.multiple_of((place[2] ^ i) * half, 16), half)], outs[i], sem.at[i]
            )
            for i in range(2)
        ]
    else:
        back = [pltpu.make_async_copy(result, outs[0], sem.at[0])]
    for one in back:
        one.start()
    for one in back:
        one.wait()


def total_of(operands, place, token, halves=False, extra=None):
    rows, depth = operands[0].shape
    given = [("smem", place)] + [("hbm", value) for value in operands]
    if extra is not None:
        given.append(("vmem", extra))
    outs = [("hbm", (rows // 2, depth), jnp.bfloat16)] * 2 if halves else [("hbm", (rows, depth), jnp.bfloat16)]
    results = call(
        functools.partial(total_body, len(operands), halves, extra is not None),
        given + [("hbm", token)],
        [("hbm", token.shape, token.dtype)] + outs,
        {len(given): 0},
        [
            pltpu.VMEM((len(operands), rows, depth), jnp.bfloat16),
            pltpu.VMEM((rows, depth), jnp.bfloat16),
            pltpu.SemaphoreType.DMA((len(operands),)),
        ],
        limit=8,
    )
    return (results[1:] if halves else results[1]), results[0]


def finish_body(start, scale, place, mine, other, *refs):
    outs = refs[-6:-4]
    ending, values, result, sem = refs[-4:]
    half, depth = mine.shape
    wide = result.shape[1]
    moves = [
        pltpu.make_async_copy(
            one, values.at[pl.ds(pl.multiple_of((place[2] ^ i) * half, 16), half)], sem.at[i]
        )
        for i, one in enumerate((mine, other))
    ]
    for one in moves:
        one.start()
    for one in moves:
        one.wait()

    @pl.loop(0, 2 * half // 16)
    def _(strip):
        here = pl.ds(pl.multiple_of(strip * 16, 16), 16)
        total = values[here, :].astype(jnp.float32) * scale
        ending[here, :] = total[:, depth - LANES :]
        result[here, :] = total[:, :wide]

    here = pl.ds(start, 2 * half)
    back = [
        pltpu.make_async_copy(result, outs[0].at[here], sem.at[0]),
        pltpu.make_async_copy(ending, outs[1].at[here], sem.at[1]),
    ]
    for one in back:
        one.start()
    for one in back:
        one.wait()


def finish_of(mine, other, results, shapes, start, scale, place, token):
    half, depth = mine.shape
    given = [("smem", place), ("hbm", mine), ("hbm", other)]
    aliases = {len(given): 0}
    given.append(("hbm", token))
    for i, value in enumerate(results):
        aliases[len(given)] = 1 + i
        given.append(("hbm", value))
    outs = call(
        functools.partial(finish_body, start, scale),
        given,
        [("hbm", token.shape, token.dtype)] + [("hbm", one, jnp.float32) for one in shapes],
        aliases,
        [
            pltpu.VMEM((2 * half, LANES), jnp.float32),
            pltpu.VMEM((2 * half, depth), jnp.bfloat16),
            pltpu.VMEM((2 * half, shapes[0][1]), jnp.float32),
            pltpu.SemaphoreType.DMA((2,)),
        ],
        limit=8,
    )
    return outs[1:], outs[0]


def gains_body(acc, plain, token, token_out, gain):
    rows2, depth = plain.shape
    gain[...] = jnp.zeros_like(gain)

    @pl.loop(0, rows2 // 16)
    def _(strip):
        here = pl.ds(pl.multiple_of(strip * 16, 16), 16)
        values = plain[here, :].astype(jnp.float32)
        x_hat = values * lax.rsqrt(jnp.mean(values * values, axis=1, keepdims=True) + 1e-06)
        product = acc[here, :depth] * x_hat
        gain[...] += product[:8] + product[8:]


def gains(acc, plain, token):
    results = call(
        gains_body,
        [("vmem", acc), ("vmem", plain), ("hbm", token)],
        [("hbm", token.shape, token.dtype), ("vmem", (8, plain.shape[1]), jnp.float32)],
        {2: 0},
    )
    return results[1], results[0]


def close_body(acc, state, token, token_out, state_out, own, peer, sem):
    rows = own.shape[0]
    out = [
        pltpu.make_async_copy(acc.at[pl.ds(0, rows)], own, sem.at[0]),
        pltpu.make_async_copy(acc.at[pl.ds(rows, rows)], peer, sem.at[1]),
    ]
    for one in out:
        one.start()
    for one in out:
        one.wait()


def close(acc, state, token):
    rows2, full = acc.shape
    half = ("hbm", (rows2 // 2, full), jnp.float32)
    results = call(
        close_body,
        [("vmem", acc), ("hbm", state), ("hbm", token)],
        [("hbm", token.shape, token.dtype), ("hbm", state.shape, state.dtype), half, half],
        {1: 1, 2: 0},
        [pltpu.SemaphoreType.DMA((2,))],
    )
    return results[1:], results[0]


def pack_body(sizes, weight, bias, token, token_out, *outs):
    depth = weight.shape[1]
    full = outs[0].shape[1]
    lane = lax.broadcasted_iota(jnp.int32, (16, LANES), 1) + (full - LANES)
    start = 0
    for size, out in zip(sizes, outs):
        out[:, :depth] = weight[pl.ds(start, size), :]
        for row in range(0, size, 16):
            column = jnp.broadcast_to(bias[:, start + row : start + row + 16], (LANES, 16)).T
            last = out[row : row + 16, full - LANES :].astype(jnp.float32)
            last = jnp.where(lane < depth, last, jnp.where(lane == depth, column, 0.0))
            out[row : row + 16, full - LANES :] = last.astype(jnp.bfloat16)
        start += size


def pack(weight, bias, token):
    depth = weight.shape[1]
    full = depth + -depth % LANES
    results = call(
        functools.partial(pack_body, CHUNKS),
        [("vmem", weight), ("vmem", bias.astype(jnp.float32)[None, :]), ("hbm", token)],
        [("hbm", token.shape, token.dtype)]
        + [("vmem", (size, full), jnp.bfloat16) for size in CHUNKS],
        {2: 0},
    )
    return results[1:], results[0]


def ranges(units, width):
    for first in range(0, units, LANES):
        at, cuts = first, []
        while at < min(first + LANES, units):
            stop = min(first + LANES, units, (at // width + 1) * width)
            cuts.append((at // width, at % width, at - first, stop - at))
            at = stop
        yield first, cuts


def turn_body(width, place, cot, cot_peer, token, token_out, own, peer):
    core = place[1]
    for source, out in ((cot, own), (cot_peer, peer)):
        for parity in range(2):

            @pl.when(core == parity)
            def _():
                for first, cuts in ranges(source.shape[1], width):
                    cuts = [cut for cut in cuts if cut[0] % 2 == parity]
                    if cuts:
                        block = source[:, first : first + LANES].T
                    for shard, offset, at, size in cuts:
                        to = pl.ds((shard // 2) * width + offset, size)
                        out[to, :] = block[at : at + size]


def turn(cotangent, cot_peer, width, place, token):
    rows, units = cotangent.shape
    half = ("vmem", (units // 2, rows), jnp.bfloat16)
    results = call(
        functools.partial(turn_body, width),
        [("smem", place), ("vmem", cotangent), ("vmem", cot_peer), ("hbm", token)],
        [("hbm", token.shape, token.dtype), half, half],
        {3: 0},
        limit=20,
    )
    return results[1:], results[0]


def back_body(width, place, own, peer, token, token_out, out):
    core = place[1]
    for first, cuts in ranges(out.shape[1], width):
        blocks = []
        for shard, offset, at, size in cuts:
            to = pl.ds((shard // 2) * width + offset, size)
            blocks.append(jnp.where(core == shard % 2, own[to, :], peer[to, :]))
        block = blocks[0] if len(blocks) == 1 else jnp.concatenate(blocks, axis=0)
        out[:, first : first + LANES] = block.T


def back(own, peer, width, place, token):
    units, rows = 2 * own.shape[0], own.shape[1]
    results = call(
        functools.partial(back_body, width),
        [("smem", place), ("vmem", own), ("vmem", peer), ("hbm", token)],
        [("hbm", token.shape, token.dtype), ("vmem", (rows, units), jnp.bfloat16)],
        {3: 0},
    )
    return results[1], results[0]


def norm_body(own, peer, gain, token, token_out, normed, flipped, plain):
    depth, rows = own.shape
    full = normed.shape[1]
    lane = lax.broadcasted_iota(jnp.int32, (LANES, LANES), 1) + (full - LANES)
    for index, source in enumerate((own, peer)):
        for strip in range(0, rows, LANES):
            to = pl.ds(index * rows + strip, LANES)
            for col in range(0, depth, LANES):
                wide = min(LANES, depth - col)
                plain[to, col : col + wide] = source[col : col + wide, strip : strip + LANES].T
            values = plain[to, :].astype(jnp.float32)
            mean_sq = jnp.mean(values * values, axis=1, keepdims=True)
            value = values * lax.rsqrt(mean_sq + 1e-06) * gain[...]
            normed[to, :depth] = value.astype(jnp.bfloat16)
            last = normed[to, full - LANES :]
            last = jnp.where(lane < depth, last, jnp.where(lane == depth, 1.0, 0.0).astype(jnp.bfloat16))
            normed[to, full - LANES :] = last
            for col in range(0, full, LANES):
                flipped[col : col + LANES, to] = normed[to, col : col + LANES].T


def norm(tokens, peer, norm_gain, token):
    depth, rows = tokens.shape
    full = depth + -depth % LANES
    results = call(
        norm_body,
        [("vmem", tokens), ("vmem", peer), ("vmem", norm_gain[None, :]), ("hbm", token)],
        [
            ("hbm", token.shape, token.dtype),
            ("vmem", (2 * rows, full), jnp.bfloat16),
            ("vmem", (full, 2 * rows), jnp.bfloat16),
            ("vmem", (2 * rows, depth), jnp.bfloat16),
        ],
        {3: 0},
        limit=16,
    )
    return results[1:], results[0]


def swap_plane(value, bit=1):
    return lax.ppermute(value, "rep", [(i, i ^ bit) for i in range(4)])


def paired(tokens, norm_gain, up_weight, up_bias, keep_mask, cotangent):
    rows, depth = tokens.shape
    width = up_weight.shape[0]
    index = lax.axis_index("fsdp")
    plane = lax.axis_index("rep")
    place = jnp.stack([index >> 1, index & 1, plane & 1]).astype(jnp.int32)
    inv_root = 1.0 / math.sqrt(rows * 32)
    count = len(CHUNKS)
    starts = [sum(CHUNKS[:c]) for c in range(count)]
    spare = -depth % LANES

    token = jnp.zeros((8, LANES), jnp.float32)
    own, token = pack(up_weight, up_bias, token)
    from_x = [swap_x(piece) for piece in own]
    from_y = [swap_y(piece) for piece in own]
    from_d = [None] * 2 + [swap_x(from_y[c]) if c % 2 == 0 else swap_y(from_x[c]) for c in range(2, count)]

    flat = tokens.T
    (normed, flipped, plain), token = norm(flat, swap_core(flat), norm_gain, token)
    scale_own = row_scales(keep_mask, rows)
    scale = jnp.concatenate([scale_own, swap_core(scale_own)])[None, :]
    states, token = turn(cotangent, swap_core(cotangent), width, place, token)

    pieces = {}
    for c in range(count):
        pieces["O", c], pieces["X", c], pieces["Y", c] = own[c], from_x[c], from_y[c]
        pieces["D", c] = from_d[c]
    side = {"O": 0, "X": 1, "Y": 2, "D": 3}
    grads, sent_x, sent_y, relayed = {}, {}, {}, {}
    kept, across, results, acc = {}, {}, (), None
    hidden = grad_in = None

    def run(keys):
        nonlocal states, token, acc
        spots = [(starts[c], side[kind]) for kind, c in keys]
        states, token, acc, grad = work(
            [pieces[key] for key in keys], spots, width, place, normed, flipped, scale, states, token, acc
        )
        grads.update(zip(keys, grad))

    for task in "".join(ORDER).split():
        kind, c = task[0], int(task[1:]) if task[1:].isdigit() else 0
        even = c % 2 == 0
        if kind == "W":
            run([("X", c), ("Y", c)])
            if even:
                sent_y[c] = swap_y(grads["Y", c])
            else:
                sent_x[c] = swap_x(grads["X", c])
        elif kind == "B":
            run([("D", c)])
            relayed[c] = swap_y(grads["D", c]) if even else swap_x(grads["D", c])
        elif kind == "O":
            run([("O", k) for k in (range(2) if task == "Oa" else range(2, count))])
        elif kind == "r":
            value, token = repeat(from_y[c] if even else from_x[c], token)
            pieces["D", c] = swap_x(value) if even else swap_y(value)
        elif kind == "R":
            value, token = total_of([grads["X" if even else "Y", c], relayed[c]], place, token)
            if even:
                sent_x[c] = swap_x(value)
            else:
                sent_y[c] = swap_y(value)
        elif kind == "S":
            extra = None
            if c == count - 1:
                lanes = gain.reshape(depth // 32, 32)
                extra = jnp.pad(lanes, ((0, CHUNKS[c] - depth // 32), (LANES - 32, 0)))
            terms = [grads["O", c], sent_x[c], sent_y[c]]
            (kept[c], other), token = total_of(terms, place, token, True, extra)
            across[c] = swap_plane(other, 1)
        elif kind == "T":
            kept[c], token = total_of([kept[c], across[c]], place, token)
            across[c] = swap_plane(kept[c], 2)
        elif kind == "V":
            kept[c], token = total_of([kept[c], across[c]], place, token)
            across[c] = swap_plane(kept[c], 1)
        elif kind == "U":
            shapes = [(width, depth), (width, LANES)]
            results, token = finish_of(
                kept[c], across[c], results, shapes, starts[c], inv_root, place, token
            )
        elif kind == "G":
            gain, token = gains(acc, plain, token)
            gain = jnp.sum(gain, axis=0)
            gain = gain + swap_core(gain)
        elif kind == "g":
            token = tie(token, gain)
            if task == "ga":
                gain = gain + swap_x(gain)
            elif task == "gb":
                gain = gain + swap_y(gain)
        elif kind == "K":
            (state, whole, peer), token = close(acc, states[1], token)
            state, peer = swap_core(state), swap_core(peer)
        elif kind == "H":
            hidden, token = back(states[0], state, width, place, token)
        elif kind == "J":
            x_hat, inv_rms, _ = normalize(plain[:rows], norm_gain)
            scaled = (whole + peer)[:, :depth] * norm_gain[None, :]
            grad_in = (
                inv_rms * (scaled - x_hat * jnp.mean(scaled * x_hat, axis=1, keepdims=True))
            ).astype(jnp.bfloat16)
            token = tie(token, grad_in)

    grad_weight, tail = results
    grad_bias = tail[:, LANES - spare]
    grad_gain = tail[starts[-1] : starts[-1] + depth // 32, LANES - 32 :].reshape(depth)
    return (hidden, grad_in, grad_weight, grad_bias, grad_gain)


def local(tokens, norm_gain, up_weight, up_bias, keep_mask, cotangent):
    x_hat, inv_rms, normed = normalize(tokens, norm_gain)
    rows = tokens.shape[0]
    width = up_weight.shape[0]
    tok_total = rows * lax.axis_size("fsdp") * lax.axis_size("rep")
    inv_root = 1.0 / math.sqrt(tok_total)
    weight_all, bias_all = (
        lax.all_gather(up_weight, "fsdp", axis=0, tiled=True),
        lax.all_gather(up_bias, "fsdp", axis=0, tiled=True),
    )
    scales = row_scales(keep_mask, rows)[:, None]
    preact = contract_last(normed, weight_all) + bias_all.astype(jnp.float32)[None, :]
    gelu_out, slopes = activate(preact)
    hidden = (gelu_out * scales).astype(jnp.bfloat16)
    grad_pre = cotangent.astype(jnp.float32) * scales * slopes
    grad_low = grad_pre.astype(jnp.bfloat16)
    weight_part = lax.psum_scatter(
        lax.dot_general(
            grad_low, normed, (((0,), (0,)), ((), ())), preferred_element_type=jnp.float32
        ).astype(jnp.bfloat16),
        "fsdp",
        scatter_dimension=0,
        tiled=True,
    )
    weight_sum = lax.psum(weight_part, "rep").astype(jnp.float32)
    grad_norm = jnp.dot(grad_low, weight_all, preferred_element_type=jnp.float32)
    bias_total, gain_total = lax.psum(
        (jnp.sum(grad_pre, axis=0), jnp.sum(grad_norm * x_hat, axis=0)), ("fsdp", "rep")
    )
    bias_sum = lax.dynamic_slice_in_dim(bias_total, lax.axis_index("fsdp") * width, width, 0)
    scaled = grad_norm * norm_gain[None, :]
    grad_in = (inv_rms * (scaled - x_hat * jnp.mean(scaled * x_hat, axis=1, keepdims=True))).astype(
        jnp.bfloat16
    )
    return (hidden, grad_in, weight_sum * inv_root, bias_sum * inv_root, gain_total * inv_root)


def solution(mesh):
    body = paired if (mesh.shape["fsdp"], mesh.shape["rep"]) == (8, 4) else local
    return jax.shard_map(
        body,
        mesh=mesh,
        in_specs=(
            P(("fsdp", "rep"), None),
            P(),
            P("fsdp", None),
            P("fsdp"),
            P(("fsdp", "rep")),
            P(("fsdp", "rep"), None),
        ),
        out_specs=(
            P(("fsdp", "rep"), None),
            P(("fsdp", "rep"), None),
            P("fsdp", None),
            P("fsdp"),
            P(),
        ),
        check_vma=False,
    )
```

profile of v0, /device:TPU:0, one launch (start us, length us, event | category | flops | bytes accessed | tf_op | source)
XLA Modules:
  0.0 274.2 jit_solution(2096296116546982630)
XLA Ops:
  18.0 3.3 %copy-done.11 = bf16[384,6400]{1,0:T(8,128)(2,1)S(1)} copy-done((bf16[384,6400]{1,0:T(8,128)(2,1)S(1)}, bf16[384,6400]{1,0:T(8,128)(2,1)}, u32[]{:S(2)}) %copy-start.11) | copy-done | bytes 4915224
  21.3 4.5 %shard_map.103 = (f32[8,128]{1,0:T(8,128)S(1)}, bf16[3200,384]{1,0:T(8,128)(2,1)S(1)}, bf16[3200,384]{1,0:T(8,128)(2,1)S(1)}) custom-call(s32[3]{0:T(128)S(1)} %pad_add_fusion.place.refs_0_, bf16[384,6400]{1,0:T(8,128)(2,1)S(1)} %copy-done.11, bf16[384,6400]{1,0:T(8,128)(2,1)} %collective-permute-done.14.cot_peer, ...), custom_call_target="tpu_custom_call", output_to_operand_aliasing={{0}: (3, {})} | custom-call | tf_op jit(solution)/shard_map/pallas_call | solution.py:152
  25.8 8.3 %shard_map.104 = (bf16[3200,384]{1,0:T(8,128)(2,1)S(1)}, bf16[3200,384]{1,0:T(8,128)(2,1)S(1)}, f32[8,128]{1,0:T(8,128)S(1)}, f32[768,1664]{1,0:T(8,128)S(1)}, b...) custom-call(s32[3]{0:T(128)S(1)} %pad_add_fusion.place.refs_0_, ...), custom_call_target="tpu_custom_call", output_to_operand_aliasing={{0}: (6, {}), {1}: (7, {}), {2}: (8, {})} | custom-call | tf_op jit(solution)/shard_map/pallas_call | solution.py:152
  36.8 8.5 %shard_map.106 = (bf16[3200,384]{1,0:T(8,128)(2,1)S(1)}, bf16[3200,384]{1,0:T(8,128)(2,1)S(1)}, f32[8,128]{1,0:T(8,128)S(1)}, f32[768,1664]{1,0:T(8,128)S(1)}, b...) custom-call(s32[3]{0:T(128)S(1)} %pad_add_fusion.place.refs_0_, ...), custom_call_target="tpu_custom_call", output_to_operand_aliasing={{0}: (6, {}), {1}: (7, {}), {2}: (8, {}), {3}: (9, {})} | custom-call | tf_op jit(solution)/shard_map/pallas_call | solution.py:152
  46.6 8.0 %shard_map.108 = (bf16[3200,384]{1,0:T(8,128)(2,1)S(1)}, bf16[3200,384]{1,0:T(8,128)(2,1)S(1)}, f32[8,128]{1,0:T(8,128)S(1)}, f32[768,1664]{1,0:T(8,128)S(1)}, b...) custom-call(s32[3]{0:T(128)S(1)} %pad_add_fusion.place.refs_0_, ...), custom_call_target="tpu_custom_call", output_to_operand_aliasing={{0}: (6, {}), {1}: (7, {}), {2}: (8, {}), {3}: (9, {})} | custom-call | tf_op jit(solution)/shard_map/pallas_call | solution.py:152
  55.4 4.4 %shard_map.109 = (bf16[3200,384]{1,0:T(8,128)(2,1)S(1)}, bf16[3200,384]{1,0:T(8,128)(2,1)S(1)}, f32[8,128]{1,0:T(8,128)S(1)}, f32[768,1664]{1,0:T(8,128)S(1)}, bf16[192,1664]{1,0:T(8,128)(2,1)S(1)}) custom-call(s32[3]{0:T(128)S(1)} %pad_add_fusion.place.refs_0_, ...), custom_call_target="tpu_custom_call", output_to_operand_aliasing={{0}: (5, {}), {1}: (6, {}), {2}: (7, {}), {3}: (8, {})} | custom-call | tf_op jit(solution)/shard_map/pallas_call | solution.py:152
  65.0 4.4 %shard_map.110 = (bf16[3200,384]{1,0:T(8,128)(2,1)S(1)}, bf16[3200,384]{1,0:T(8,128)(2,1)S(1)}, f32[8,128]{1,0:T(8,128)S(1)}, f32[768,1664]{1,0:T(8,128)S(1)}, bf16[192,1664]{1,0:T(8,128)(2,1)S(1)}) custom-call(s32[3]{0:T(128)S(1)} %pad_add_fusion.place.refs_0_, ...), custom_call_target="tpu_custom_call", output_to_operand_aliasing={{0}: (5, {}), {1}: (6, {}), {2}: (7, {}), {3}: (8, {})} | custom-call | tf_op jit(solution)/shard_map/pallas_call | solution.py:152
  77.0 6.8 %shard_map.111 = (bf16[3200,384]{1,0:T(8,128)(2,1)S(1)}, bf16[3200,384]{1,0:T(8,128)(2,1)S(1)}, f32[8,128]{1,0:T(8,128)S(1)}, f32[768,1664]{1,0:T(8,128)S(1)}, b...) custom-call(s32[3]{0:T(128)S(1)} %pad_add_fusion.place.refs_0_, ...), custom_call_target="tpu_custom_call", output_to_operand_aliasing={{0}: (6, {}), {1}: (7, {}), {2}: (8, {}), {3}: (9, {})} | custom-call | tf_op jit(solution)/shard_map/pallas_call | solution.py:152
  86.6 4.2 %shard_map.112 = (bf16[3200,384]{1,0:T(8,128)(2,1)S(1)}, bf16[3200,384]{1,0:T(8,128)(2,1)S(1)}, f32[8,128]{1,0:T(8,128)S(1)}, f32[768,1664]{1,0:T(8,128)S(1)}, bf16[160,1664]{1,0:T(8,128)(2,1)S(1)}) custom-call(s32[3]{0:T(128)S(1)} %pad_add_fusion.place.refs_0_, ...), custom_call_target="tpu_custom_call", output_to_operand_aliasing={{0}: (5, {}), {1}: (6, {}), {2}: (7, {}), {3}: (8, {})} | custom-call | tf_op jit(solution)/shard_map/pallas_call | solution.py:152
  94.3 6.0 %collective-permute-done.18.refs_2_ = bf16[192,1664]{1,0:T(8,128)(2,1)S(1)} collective-permute-done((bf16[192,1664]{1,0:T(8,128)(2,1)S(1)}, bf16[192,1664]{1,0:T(8,128)(2,1)S(1)}, u32[]{:S(2)}, u32[]{:S(2)}) %collective-permute-start.18) | collective-permute-done | bytes 639008 | tf_op jit(solution)/shard_map/ppermute | solution.py:54
  103.5 8.2 %collective-permute-done.5.refs_4_ = bf16[160,1664]{1,0:T(8,128)(2,1)S(1)} collective-permute-done((bf16[160,1664]{1,0:T(8,128)(2,1)S(1)}, bf16[160,1664]{1,0:T(8,128)(2,1)S(1)}, u32[]{:S(2)}, u32[]{:S(2)}) %collective-permute-start.5) | collective-permute-done | bytes 532512 | tf_op jit(solution)/shard_map/ppermute | solution.py:54
  113.8 8.5 %shard_map.115 = (bf16[3200,384]{1,0:T(8,128)(2,1)S(1)}, bf16[3200,384]{1,0:T(8,128)(2,1)S(1)}, f32[8,128]{1,0:T(8,128)S(1)}, f32[768,1664]{1,0:T(8,128)S(1)}, b...) custom-call(s32[3]{0:T(128)S(1)} %pad_add_fusion.place.refs_0_, ...), custom_call_target="tpu_custom_call", output_to_operand_aliasing={{0}: (7, {}), {1}: (8, {}), {2}: (9, {}), {3}: (10, {})} | custom-call | tf_op jit(solution)/shard_map/pallas_call | solution.py:152
  122.2 3.2 %collective-permute-done.20.refs_2_ = bf16[192,1664]{1,0:T(8,128)(2,1)S(1)} collective-permute-done((bf16[192,1664]{1,0:T(8,128)(2,1)S(1)}, bf16[192,1664]{1,0:T(8,128)(2,1)S(1)}, u32[]{:S(2)}, u32[]{:S(2)}) %collective-permute-start.20) | collective-permute-done | bytes 639008 | tf_op jit(solution)/shard_map/ppermute | solution.py:54
  128.9 8.7 %collective-permute-done.23.refs_2_ = bf16[192,1664]{1,0:T(8,128)(2,1)S(1)} collective-permute-done((bf16[192,1664]{1,0:T(8,128)(2,1)S(1)}, bf16[192,1664]{1,0:T(8,128)(2,1)S(1)}, u32[]{:S(2)}, u32[]{:S(2)}) %collective-permute-start.23) | collective-permute-done | bytes 639008 | tf_op jit(solution)/shard_map/ppermute | solution.py:54
  148.1 6.7 %shard_map.119 = (bf16[3200,384]{1,0:T(8,128)(2,1)S(1)}, bf16[3200,384]{1,0:T(8,128)(2,1)S(1)}, f32[8,128]{1,0:T(8,128)S(1)}, f32[768,1664]{1,0:T(8,128)S(1)}, b...) custom-call(s32[3]{0:T(128)S(1)} %pad_add_fusion.place.refs_0_, ...), custom_call_target="tpu_custom_call", output_to_operand_aliasing={{0}: (6, {}), {1}: (7, {}), {2}: (8, {}), {3}: (9, {})} | custom-call | tf_op jit(solution)/shard_map/pallas_call | solution.py:152
  154.8 4.4 %shard_map.120 = (bf16[3200,384]{1,0:T(8,128)(2,1)S(1)}, bf16[3200,384]{1,0:T(8,128)(2,1)S(1)}, f32[8,128]{1,0:T(8,128)S(1)}, f32[768,1664]{1,0:T(8,128)S(1)}, bf16[160,1664]{1,0:T(8,128)(2,1)S(1)}) custom-call(s32[3]{0:T(128)S(1)} %pad_add_fusion.place.refs_0_, ...), custom_call_target="tpu_custom_call", output_to_operand_aliasing={{0}: (5, {}), {1}: (6, {}), {2}: (7, {}), {3}: (8, {})} | custom-call | tf_op jit(solution)/shard_map/pallas_call | solution.py:152
  162.9 5.1 %shard_map.121 = (bf16[3200,384]{1,0:T(8,128)(2,1)S(1)}, bf16[3200,384]{1,0:T(8,128)(2,1)S(1)}, f32[8,128]{1,0:T(8,128)S(1)}, f32[768,1664]{1,0:T(8,128)S(1)}, b...) custom-call(s32[3]{0:T(128)S(1)} %pad_add_fusion.place.refs_0_, ...), custom_call_target="tpu_custom_call", output_to_operand_aliasing={{0}: (6, {}), {1}: (7, {}), {2}: (8, {}), {3}: (9, {})} | custom-call | tf_op jit(solution)/shard_map/pallas_call | solution.py:152
  172.5 8.7 %collective-permute-done.3.refs_4_ = bf16[96,1664]{1,0:T(8,128)(2,1)S(1)} collective-permute-done((bf16[96,1664]{1,0:T(8,128)(2,1)S(1)}, bf16[96,1664]{1,0:T(8,128)(2,1)S(1)}, u32[]{:S(2)}, u32[]{:S(2)}) %collective-permute-start.3) | collective-permute-done | bytes 319520 | tf_op jit(solution)/shard_map/ppermute | solution.py:54
  181.7 3.4 %shard_map.125 = (bf16[3200,384]{1,0:T(8,128)(2,1)S(1)}, bf16[3200,384]{1,0:T(8,128)(2,1)S(1)}, f32[8,128]{1,0:T(8,128)S(1)}, f32[768,1664]{1,0:T(8,128)S(1)}, bf16[96,1664]{1,0:T(8,128)(2,1)}) custom-call(s32[3]{0:T(128)S(1)} %pad_add_fusion.place.refs_0_, ...), custom_call_target="tpu_custom_call", output_to_operand_aliasing={{0}: (5, {}), {1}: (6, {}), {2}: (7, {}), {3}: (8, {})} | custom-call | tf_op jit(solution)/shard_map/pallas_call | solution.py:152
  191.8 5.4 %shard_map.128 = (f32[8,128]{1,0:T(8,128)S(1)}, f32[8,1600]{1,0:T(8,128)S(1)}) custom-call(f32[768,1664]{1,0:T(8,128)S(1)} %get-tuple-element.243.acc, bf16[768,1600]{1,0:T(8,128)(2,1)S(1)} %get-tuple-element.251.plain, f32[8,128]{1,0:T(8,128)S(1)} %get-tuple-element.254.token), custom_call_target="tpu_custom_call", output_to_operand_aliasing={{0}: (2, {})} | custom-call | tf_op jit(solution)/shard_map/pallas_call | solution.py:152
  235.7 4.1 %collective-permute-done.47.other = bf16[80,1664]{1,0:T(8,128)(2,1)} collective-permute-done((bf16[80,1664]{1,0:T(8,128)(2,1)}, bf16[80,1664]{1,0:T(8,128)(2,1)}, u32[]{:S(2)}, u32[]{:S(2)}) %collective-permute-start.47) | collective-permute-done | bytes 266272 | tf_op jit(solution)/shard_map/ppermute | solution.py:518
  251.7 3.0 %collective-permute-start.52 = (bf16[80,1664]{1,0:T(8,128)(2,1)S(1)}, bf16[80,1664]{1,0:T(8,128)(2,1)S(1)}, u32[]{:S(2)}, u32[]{:S(2)}) collective-permute-start(bf16[80,1664]{1,0:T(8,128)(2,1)S(1)} %get-tuple-element.300.mine), channel_id=1, source_target_pairs={{0,1},{1,0},{2,3},{3,2},{4,5},{5,4},{6,7},{7,6},{8,9},{9,8},{10,11... | collective-permute-start | bytes 798728 | tf_op jit(solution)/shard_map/ppermute | solution.py:518
  254.7 5.2 %collective-permute-done.49.refs_2_ = bf16[48,1664]{1,0:T(8,128)(2,1)S(1)} collective-permute-done((bf16[48,1664]{1,0:T(8,128)(2,1)S(1)}, bf16[48,1664]{1,0:T(8,128)(2,1)S(1)}, u32[]{:S(2)}, u32[]{:S(2)}) %collective-permute-start.49) | collective-permute-done | bytes 159776 | tf_op jit(solution)/shard_map/ppermute | solution.py:518
  261.4 4.1 %shard_map.146 = (f32[8,128]{1,0:T(8,128)S(1)}, bf16[384,6400]{1,0:T(8,128)(2,1)}) custom-call(s32[3]{0:T(128)S(1)} %pad_add_fusion.place.refs_0_, bf16[3200,384]{1,0:T(8,128)(2,1)S(1)} %get-tuple-element.242.own, bf16[3200,384]{1,0:T(8,128)(2,1)S(1)} %collective-permute-done.48.peer, ...), custom_call_target="tpu_custom_call", output_to_operand_aliasing={{0}: (3, {})} | custom-call | tf_op jit(solution)/shard_map/pallas_call | solution.py:152
  (218 shorter events, 135.5 us)
Async XLA Ops:
  7.9 26.2 %collective-permute-start.13 = (bf16[192,1664]{1,0:T(8,128)(2,1)}, bf16[192,1664]{1,0:T(8,128)(2,1)}, u32[]{:S(2)}, u32[]{:S(2)}) collective-permute-start(bf16[192,1664]{1,0:T(8,128)(2,1)} %get-tuple-element.164.refs_4_), channel_id=1, source_target_pairs={{0,16},{4,20},{8,24},{12,28},{16,0},{20,4},{24,8},{28,12},{1,17},{... | collective-permute-start | bytes 1916936 | tf_op jit(solution)/shard_map/ppermute | solution.py:54
  11.0 25.8 %collective-permute-start.12 = (bf16[192,1664]{1,0:T(8,128)(2,1)}, bf16[192,1664]{1,0:T(8,128)(2,1)}, u32[]{:S(2)}, u32[]{:S(2)}) collective-permute-start(bf16[192,1664]{1,0:T(8,128)(2,1)} %get-tuple-element.164.refs_4_), channel_id=1, source_target_pairs={{0,8},{4,12},{8,0},{12,4},{16,24},{20,28},{24,16},{28,20},{1,9},{5... | collective-permute-start | bytes 1916936 | tf_op jit(solution)/shard_map/ppermute | solution.py:54
  12.6 32.7 %collective-permute-start.11 = (bf16[192,1664]{1,0:T(8,128)(2,1)}, bf16[192,1664]{1,0:T(8,128)(2,1)S(1)}, u32[]{:S(2)}, u32[]{:S(2)}) collective-permute-start(bf16[192,1664]{1,0:T(8,128)(2,1)} %copy-done.14), channel_id=1, source_target_pairs={{0,8},{4,12},{8,0},{12,4},{16,24},{20,28},{24,16},{28,20},{1,9},{5... | collective-permute-start | bytes 1916936 | tf_op jit(solution)/shard_map/ppermute | solution.py:54
  13.8 32.9 %collective-permute-start.17 = (bf16[192,1664]{1,0:T(8,128)(2,1)}, bf16[192,1664]{1,0:T(8,128)(2,1)S(1)}, u32[]{:S(2)}, u32[]{:S(2)}) collective-permute-start(bf16[192,1664]{1,0:T(8,128)(2,1)} %copy-done.14), channel_id=1, source_target_pairs={{0,16},{4,20},{8,24},{12,28},{16,0},{20,4},{24,8},{28,12},{1,17},{... | collective-permute-start | bytes 1916936 | tf_op jit(solution)/shard_map/ppermute | solution.py:54
  35.8 26.1 %collective-permute-start.8 = (bf16[160,1664]{1,0:T(8,128)(2,1)S(1)}, bf16[160,1664]{1,0:T(8,128)(2,1)S(1)}, u32[]{:S(2)}, u32[]{:S(2)}) collective-permute-start(bf16[160,1664]{1,0:T(8,128)(2,1)S(1)} %copy-done.19), channel_id=1, source_target_pairs={{0,16},{4,20},{8,24},{12,28},{16,0},{20,4},{24,8},{28,12},{1,17},{... | collective-permute-start | bytes 1597448 | tf_op jit(solution)/shard_map/ppermute | solution.py:54
  59.9 31.0 %collective-permute-start.19 = (bf16[192,1664]{1,0:T(8,128)(2,1)S(1)}, bf16[192,1664]{1,0:T(8,128)(2,1)S(1)}, u32[]{:S(2)}, u32[]{:S(2)}) collective-permute-start(bf16[192,1664]{1,0:T(8,128)(2,1)S(1)} %get-tuple-element.202), channel_id=1, source_target_pairs={{0,16},{4,20},{8,24},{12,28},{16,0},{20,4},{24,8},{28,12},{1,17},{... | collective-permute-start | bytes 1916936 | tf_op jit(solution)/shard_map/ppermute | solution.py:54
  61.9 24.7 %collective-permute-start.9 = (bf16[160,1664]{1,0:T(8,128)(2,1)S(1)}, bf16[160,1664]{1,0:T(8,128)(2,1)S(1)}, u32[]{:S(2)}, u32[]{:S(2)}) collective-permute-start(bf16[160,1664]{1,0:T(8,128)(2,1)S(1)} %collective-permute-done.8.refs_5_), channel_id=1, source_target_pairs={{0,8},{4,12},{8,0},{12,4},{16,24},{20,28},{24,16},{28,20},{1,9},{5... | collective-permute-start | bytes 1597448 | tf_op jit(solution)/shard_map/ppermute | solution.py:54
  69.5 30.8 %collective-permute-start.18 = (bf16[192,1664]{1,0:T(8,128)(2,1)S(1)}, bf16[192,1664]{1,0:T(8,128)(2,1)S(1)}, u32[]{:S(2)}, u32[]{:S(2)}) collective-permute-start(bf16[192,1664]{1,0:T(8,128)(2,1)S(1)} %get-tuple-element.200), channel_id=1, source_target_pairs={{0,8},{4,12},{8,0},{12,4},{16,24},{20,28},{24,16},{28,20},{1,9},{5... | collective-permute-start | bytes 1916936 | tf_op jit(solution)/shard_map/ppermute | solution.py:54
  71.6 41.9 %collective-permute-start.21 = (bf16[192,1664]{1,0:T(8,128)(2,1)S(1)}, bf16[192,1664]{1,0:T(8,128)(2,1)S(1)}, u32[]{:S(2)}, u32[]{:S(2)}) collective-permute-start(bf16[192,1664]{1,0:T(8,128)(2,1)S(1)} %get-tuple-element.211), channel_id=1, source_target_pairs={{0,16},{4,20},{8,24},{12,28},{16,0},{20,4},{24,8},{28,12},{1,17},{... | collective-permute-start | bytes 1916936 | tf_op jit(solution)/shard_map/ppermute | solution.py:54
  75.2 36.5 %collective-permute-start.5 = (bf16[160,1664]{1,0:T(8,128)(2,1)S(1)}, bf16[160,1664]{1,0:T(8,128)(2,1)S(1)}, u32[]{:S(2)}, u32[]{:S(2)}) collective-permute-start(bf16[160,1664]{1,0:T(8,128)(2,1)S(1)} %copy-done.17), channel_id=1, source_target_pairs={{0,8},{4,12},{8,0},{12,4},{16,24},{20,28},{24,16},{28,20},{1,9},{5... | collective-permute-start | bytes 1597448 | tf_op jit(solution)/shard_map/ppermute | solution.py:54
  92.2 33.2 %collective-permute-start.20 = (bf16[192,1664]{1,0:T(8,128)(2,1)S(1)}, bf16[192,1664]{1,0:T(8,128)(2,1)S(1)}, u32[]{:S(2)}, u32[]{:S(2)}) collective-permute-start(bf16[192,1664]{1,0:T(8,128)(2,1)S(1)} %get-tuple-element.210), channel_id=1, source_target_pairs={{0,8},{4,12},{8,0},{12,4},{16,24},{20,28},{24,16},{28,20},{1,9},{5... | collective-permute-start | bytes 1916936 | tf_op jit(solution)/shard_map/ppermute | solution.py:54
  94.0 43.6 %collective-permute-start.23 = (bf16[192,1664]{1,0:T(8,128)(2,1)S(1)}, bf16[192,1664]{1,0:T(8,128)(2,1)S(1)}, u32[]{:S(2)}, u32[]{:S(2)}) collective-permute-start(bf16[192,1664]{1,0:T(8,128)(2,1)S(1)} %get-tuple-element.216), channel_id=1, source_target_pairs={{0,8},{4,12},{8,0},{12,4},{16,24},{20,28},{24,16},{28,20},{1,9},{5... | collective-permute-start | bytes 1916936 | tf_op jit(solution)/shard_map/ppermute | solution.py:54
  101.7 37.6 %collective-permute-start.24 = (bf16[192,1664]{1,0:T(8,128)(2,1)S(1)}, bf16[192,1664]{1,0:T(8,128)(2,1)S(1)}, u32[]{:S(2)}, u32[]{:S(2)}) collective-permute-start(bf16[192,1664]{1,0:T(8,128)(2,1)S(1)} %get-tuple-element.217), channel_id=1, source_target_pairs={{0,16},{4,20},{8,24},{12,28},{16,0},{20,4},{24,8},{28,12},{1,17},{... | collective-permute-start | bytes 1916936 | tf_op jit(solution)/shard_map/ppermute | solution.py:54
  111.7 32.1 %collective-permute-start.7 = (bf16[160,1664]{1,0:T(8,128)(2,1)S(1)}, bf16[160,1664]{1,0:T(8,128)(2,1)S(1)}, u32[]{:S(2)}, u32[]{:S(2)}) collective-permute-start(bf16[160,1664]{1,0:T(8,128)(2,1)S(1)} %copy-done.17), channel_id=1, source_target_pairs={{0,16},{4,20},{8,24},{12,28},{16,0},{20,4},{24,8},{28,12},{1,17},{... | collective-permute-start | bytes 1597448 | tf_op jit(solution)/shard_map/ppermute | solution.py:54
  113.5 33.0 %collective-permute-start.6 = (bf16[160,1664]{1,0:T(8,128)(2,1)S(1)}, bf16[160,1664]{1,0:T(8,128)(2,1)S(1)}, u32[]{:S(2)}, u32[]{:S(2)}) collective-permute-start(bf16[160,1664]{1,0:T(8,128)(2,1)S(1)} %collective-permute-done.5.refs_4_), channel_id=1, source_target_pairs={{0,16},{4,20},{8,24},{12,28},{16,0},{20,4},{24,8},{28,12},{1,17},{... | collective-permute-start | bytes 1597448 | tf_op jit(solution)/shard_map/ppermute | solution.py:54
  137.6 21.6 %collective-permute-start.2 = (bf16[96,1664]{1,0:T(8,128)(2,1)S(1)}, bf16[96,1664]{1,0:T(8,128)(2,1)S(1)}, u32[]{:S(2)}, u32[]{:S(2)}) collective-permute-start(bf16[96,1664]{1,0:T(8,128)(2,1)S(1)} %get-tuple-element.160.refs_6_), channel_id=1, source_target_pairs={{0,16},{4,20},{8,24},{12,28},{16,0},{20,4},{24,8},{28,12},{1,17},{... | collective-permute-start | bytes 958472 | tf_op jit(solution)/shard_map/ppermute | solution.py:54
  139.2 31.3 %collective-permute-start.25 = (bf16[160,1664]{1,0:T(8,128)(2,1)S(1)}, bf16[160,1664]{1,0:T(8,128)(2,1)S(1)}, u32[]{:S(2)}, u32[]{:S(2)}) collective-permute-start(bf16[160,1664]{1,0:T(8,128)(2,1)S(1)} %get-tuple-element.233), channel_id=1, source_target_pairs={{0,16},{4,20},{8,24},{12,28},{16,0},{20,4},{24,8},{28,12},{1,17},{... | collective-permute-start | bytes 1597448 | tf_op jit(solution)/shard_map/ppermute | solution.py:54
  139.7 20.2 %collective-permute-start.4 = (bf16[96,1664]{1,0:T(8,128)(2,1)S(1)}, bf16[96,1664]{1,0:T(8,128)(2,1)S(1)}, u32[]{:S(2)}, u32[]{:S(2)}) collective-permute-start(bf16[96,1664]{1,0:T(8,128)(2,1)S(1)} %get-tuple-element.160.refs_6_), channel_id=1, source_target_pairs={{0,8},{4,12},{8,0},{12,4},{16,24},{20,28},{24,16},{28,20},{1,9},{5... | collective-permute-start | bytes 958472 | tf_op jit(solution)/shard_map/ppermute | solution.py:54
  146.5 22.5 %collective-permute-start.26 = (bf16[96,1664]{1,0:T(8,128)(2,1)S(1)}, bf16[96,1664]{1,0:T(8,128)(2,1)S(1)}, u32[]{:S(2)}, u32[]{:S(2)}) collective-permute-start(bf16[96,1664]{1,0:T(8,128)(2,1)S(1)} %get-tuple-element.235), channel_id=1, source_target_pairs={{0,1},{1,0},{2,3},{3,2},{4,5},{5,4},{6,7},{7,6},{8,9},{9,8},{10,11... | collective-permute-start | bytes 958472 | tf_op jit(solution)/shard_map/ppermute | solution.py:518
  159.3 25.9 %collective-permute-start.29 = (bf16[160,1664]{1,0:T(8,128)(2,1)S(1)}, bf16[160,1664]{1,0:T(8,128)(2,1)S(1)}, u32[]{:S(2)}, u32[]{:S(2)}) collective-permute-start(bf16[160,1664]{1,0:T(8,128)(2,1)S(1)} %get-tuple-element.248), channel_id=1, source_target_pairs={{0,8},{4,12},{8,0},{12,4},{16,24},{20,28},{24,16},{28,20},{1,9},{5... | collective-permute-start | bytes 1597448 | tf_op jit(solution)/shard_map/ppermute | solution.py:54
  159.9 29.1 %collective-permute-start.34 = (bf16[160,1664]{1,0:T(8,128)(2,1)S(1)}, bf16[160,1664]{1,0:T(8,128)(2,1)S(1)}, u32[]{:S(2)}, u32[]{:S(2)}) collective-permute-start(bf16[160,1664]{1,0:T(8,128)(2,1)S(1)} %get-tuple-element.258), channel_id=1, source_target_pairs={{0,16},{4,20},{8,24},{12,28},{16,0},{20,4},{24,8},{28,12},{1,17},{... | collective-permute-start | bytes 1597448 | tf_op jit(solution)/shard_map/ppermute | solution.py:54
  171.4 25.8 %collective-permute-start.33 = (bf16[160,1664]{1,0:T(8,128)(2,1)S(1)}, bf16[160,1664]{1,0:T(8,128)(2,1)S(1)}, u32[]{:S(2)}, u32[]{:S(2)}) collective-permute-start(bf16[160,1664]{1,0:T(8,128)(2,1)S(1)} %get-tuple-element.257), channel_id=1, source_target_pairs={{0,8},{4,12},{8,0},{12,4},{16,24},{20,28},{24,16},{28,20},{1,9},{5... | collective-permute-start | bytes 1597448 | tf_op jit(solution)/shard_map/ppermute | solution.py:54
  181.2 32.0 %collective-permute-start.28 = (bf16[160,1664]{1,0:T(8,128)(2,1)}, bf16[160,1664]{1,0:T(8,128)(2,1)S(1)}, u32[]{:S(2)}, u32[]{:S(2)}) collective-permute-start(bf16[160,1664]{1,0:T(8,128)(2,1)} %get-tuple-element.246), channel_id=1, source_target_pairs={{0,8},{4,12},{8,0},{12,4},{16,24},{20,28},{24,16},{28,20},{1,9},{5... | collective-permute-start | bytes 1597448 | tf_op jit(solution)/shard_map/ppermute | solution.py:54
  187.4 25.8 %collective-permute-start.30 = (bf16[160,1664]{1,0:T(8,128)(2,1)}, bf16[160,1664]{1,0:T(8,128)(2,1)}, u32[]{:S(2)}, u32[]{:S(2)}) collective-permute-start(bf16[160,1664]{1,0:T(8,128)(2,1)} %get-tuple-element.250), channel_id=1, source_target_pairs={{0,16},{4,20},{8,24},{12,28},{16,0},{20,4},{24,8},{28,12},{1,17},{... | collective-permute-start | bytes 1597448 | tf_op jit(solution)/shard_map/ppermute | solution.py:54
  (60 other events, 738.8 us)
where the time goes:
time: 280 us; the launch traced here: 274 us
  Pallas kernels  136 us (49%)
  starting transfers between devices  61.6 us (22%)
  waiting for transfers between devices  53.4 us (19%)
  local copies, waits for them, and re-layouts  19.4 us (7%)
    pallas_call x49, Pallas kernels, call(): pl.pallas_call(body, out_shape=[jax.ShapeDtypeStruct(shape, dtype) for _,...  136 us
    ppermute x38, waiting for transfers between devices, swap(): return lax.ppermute(value, 'fsdp', [(i, i ^ bit) for i in range(8)])  44.1 us
    ppermute x38, starting transfers between devices, swap(): return lax.ppermute(value, 'fsdp', [(i, i ^ bit) for i in range(8)])  41.2 us
    ppermute x15, starting transfers between devices, swap_plane(): return lax.ppermute(value, 'rep', [(i, i ^ bit) for i in range(4)])  20.4 us
    unnamed x63, local copies, waits for them, and re-layouts  16.7 us
    ppermute x15, waiting for transfers between devices, swap_plane(): return lax.ppermute(value, 'rep', [(i, i ^ bit) for i in range(4)])  9.29 us
  transfers between devices with their start and end apart: 53, of which 12 were waited for; matrix products, arithmetic and copies ran while one was open for 1% of the time, Pallas kernels for 48%

commit v1 on v0

--- a/solution.py
+++ b/solution.py
@@ -19,7 +19,7 @@
     "G S2 V1 R4 ",
     "T2 ga S3 U1 ",
     "gb V2 gd T3 ",
-    "S4 U2 T4 V3 ",
+    "S4 V3 T4 U2 ",
     "K V4 H J ",
     "U3 U4 ",
 )

time: 280 us -> 285 us (1.018)
  waiting for transfers between devices: 53.4 us -> 61.8 us
  starting transfers between devices: 61.6 us -> 58.3 us
    ppermute x15, waiting for transfers between devices: 9.29 us -> 14.5 us  [swap_plane(): return lax.ppermute(value, 'rep', [(i, i ^ bit) for i in range(4)])]
    ppermute x38, waiting for transfers between devices: 44.1 us -> 47.3 us  [swap(): return lax.ppermute(value, 'fsdp', [(i, i ^ bit) for i in range(8)])]
  transfers between devices with their start and end apart: 53 -> 53, of which waited for: 12 -> 14; matrix products, arithmetic and copies ran while one was open for 1% -> 1% of each run, Pallas kernels for 48% -> 46%
where the time goes in v1:
time: 285 us; the launch traced here: 279 us
  Pallas kernels  136 us (48%)
  waiting for transfers between devices  61.8 us (22%)
  starting transfers between devices  58.3 us (20%)
  local copies, waits for them, and re-layouts  19.4 us (7%)
    pallas_call x49, Pallas kernels, call(): pl.pallas_call(body, out_shape=[jax.ShapeDtypeStruct(shape, dtype) for _,...  136 us
    ppermute x38, waiting for transfers between devices, swap(): return lax.ppermute(value, 'fsdp', [(i, i ^ bit) for i in range(8)])  47.3 us
    ppermute x38, starting transfers between devices, swap(): return lax.ppermute(value, 'fsdp', [(i, i ^ bit) for i in range(8)])  40.1 us
    ppermute x15, starting transfers between devices, swap_plane(): return lax.ppermute(value, 'rep', [(i, i ^ bit) for i in range(4)])  18.2 us
    unnamed x63, local copies, waits for them, and re-layouts  16.7 us
    ppermute x15, waiting for transfers between devices, swap_plane(): return lax.ppermute(value, 'rep', [(i, i ^ bit) for i in range(4)])  14.5 us
  transfers between devices with their start and end apart: 53, of which 14 were waited for; matrix products, arithmetic and copies ran while one was open for 1% of the time, Pallas kernels for 46%

profile of v1, /device:TPU:0, one launch (start us, length us, event | category | flops | bytes accessed | tf_op | source)
XLA Modules:
  0.0 279.4 jit_solution(16659511509985306665)
XLA Ops:
  7.9 2.9 %collective-permute-start.13 = (bf16[192,1664]{1,0:T(8,128)(2,1)}, bf16[192,1664]{1,0:T(8,128)(2,1)}, u32[]{:S(2)}, u32[]{:S(2)}) collective-permute-start(bf16[192,1664]{1,0:T(8,128)(2,1)} %get-tuple-element.164.refs_4_), channel_id=1, source_target_pairs={{0,16},{4,20},{8,24},{12,28},{16,0},{20,4},{24,8},{28,12},{1,17},{... | collective-permute-start | bytes 1916936 | tf_op jit(solution)/shard_map/ppermute | solution.py:54
  18.0 3.3 %copy-done.11 = bf16[384,6400]{1,0:T(8,128)(2,1)S(1)} copy-done((bf16[384,6400]{1,0:T(8,128)(2,1)S(1)}, bf16[384,6400]{1,0:T(8,128)(2,1)}, u32[]{:S(2)}) %copy-start.11) | copy-done | bytes 4915224
  21.3 4.5 %shard_map.103 = (f32[8,128]{1,0:T(8,128)S(1)}, bf16[3200,384]{1,0:T(8,128)(2,1)S(1)}, bf16[3200,384]{1,0:T(8,128)(2,1)S(1)}) custom-call(s32[3]{0:T(128)S(1)} %pad_add_fusion.place.refs_0_, bf16[384,6400]{1,0:T(8,128)(2,1)S(1)} %copy-done.11, bf16[384,6400]{1,0:T(8,128)(2,1)} %collective-permute-done.14.cot_peer, ...), custom_call_target="tpu_custom_call", output_to_operand_aliasing={{0}: (3, {})} | custom-call | tf_op jit(solution)/shard_map/pallas_call | solution.py:152
  25.8 8.3 %shard_map.104 = (bf16[3200,384]{1,0:T(8,128)(2,1)S(1)}, bf16[3200,384]{1,0:T(8,128)(2,1)S(1)}, f32[8,128]{1,0:T(8,128)S(1)}, f32[768,1664]{1,0:T(8,128)S(1)}, b...) custom-call(s32[3]{0:T(128)S(1)} %pad_add_fusion.place.refs_0_, ...), custom_call_target="tpu_custom_call", output_to_operand_aliasing={{0}: (6, {}), {1}: (7, {}), {2}: (8, {})} | custom-call | tf_op jit(solution)/shard_map/pallas_call | solution.py:152
  36.8 8.5 %shard_map.106 = (bf16[3200,384]{1,0:T(8,128)(2,1)S(1)}, bf16[3200,384]{1,0:T(8,128)(2,1)S(1)}, f32[8,128]{1,0:T(8,128)S(1)}, f32[768,1664]{1,0:T(8,128)S(1)}, b...) custom-call(s32[3]{0:T(128)S(1)} %pad_add_fusion.place.refs_0_, ...), custom_call_target="tpu_custom_call", output_to_operand_aliasing={{0}: (6, {}), {1}: (7, {}), {2}: (8, {}), {3}: (9, {})} | custom-call | tf_op jit(solution)/shard_map/pallas_call | solution.py:152
  46.6 8.0 %shard_map.108 = (bf16[3200,384]{1,0:T(8,128)(2,1)S(1)}, bf16[3200,384]{1,0:T(8,128)(2,1)S(1)}, f32[8,128]{1,0:T(8,128)S(1)}, f32[768,1664]{1,0:T(8,128)S(1)}, b...) custom-call(s32[3]{0:T(128)S(1)} %pad_add_fusion.place.refs_0_, ...), custom_call_target="tpu_custom_call", output_to_operand_aliasing={{0}: (6, {}), {1}: (7, {}), {2}: (8, {}), {3}: (9, {})} | custom-call | tf_op jit(solution)/shard_map/pallas_call | solution.py:152
  55.4 4.4 %shard_map.109 = (bf16[3200,384]{1,0:T(8,128)(2,1)S(1)}, bf16[3200,384]{1,0:T(8,128)(2,1)S(1)}, f32[8,128]{1,0:T(8,128)S(1)}, f32[768,1664]{1,0:T(8,128)S(1)}, bf16[192,1664]{1,0:T(8,128)(2,1)S(1)}) custom-call(s32[3]{0:T(128)S(1)} %pad_add_fusion.place.refs_0_, ...), custom_call_target="tpu_custom_call", output_to_operand_aliasing={{0}: (5, {}), {1}: (6, {}), {2}: (7, {}), {3}: (8, {})} | custom-call | tf_op jit(solution)/shard_map/pallas_call | solution.py:152
  65.0 4.4 %shard_map.110 = (bf16[3200,384]{1,0:T(8,128)(2,1)S(1)}, bf16[3200,384]{1,0:T(8,128)(2,1)S(1)}, f32[8,128]{1,0:T(8,128)S(1)}, f32[768,1664]{1,0:T(8,128)S(1)}, bf16[192,1664]{1,0:T(8,128)(2,1)S(1)}) custom-call(s32[3]{0:T(128)S(1)} %pad_add_fusion.place.refs_0_, ...), custom_call_target="tpu_custom_call", output_to_operand_aliasing={{0}: (5, {}), {1}: (6, {}), {2}: (7, {}), {3}: (8, {})} | custom-call | tf_op jit(solution)/shard_map/pallas_call | solution.py:152
  77.0 6.8 %shard_map.111 = (bf16[3200,384]{1,0:T(8,128)(2,1)S(1)}, bf16[3200,384]{1,0:T(8,128)(2,1)S(1)}, f32[8,128]{1,0:T(8,128)S(1)}, f32[768,1664]{1,0:T(8,128)S(1)}, b...) custom-call(s32[3]{0:T(128)S(1)} %pad_add_fusion.place.refs_0_, ...), custom_call_target="tpu_custom_call", output_to_operand_aliasing={{0}: (6, {}), {1}: (7, {}), {2}: (8, {}), {3}: (9, {})} | custom-call | tf_op jit(solution)/shard_map/pallas_call | solution.py:152
  86.6 4.2 %shard_map.112 = (bf16[3200,384]{1,0:T(8,128)(2,1)S(1)}, bf16[3200,384]{1,0:T(8,128)(2,1)S(1)}, f32[8,128]{1,0:T(8,128)S(1)}, f32[768,1664]{1,0:T(8,128)S(1)}, bf16[160,1664]{1,0:T(8,128)(2,1)S(1)}) custom-call(s32[3]{0:T(128)S(1)} %pad_add_fusion.place.refs_0_, ...), custom_call_target="tpu_custom_call", output_to_operand_aliasing={{0}: (5, {}), {1}: (6, {}), {2}: (7, {}), {3}: (8, {})} | custom-call | tf_op jit(solution)/shard_map/pallas_call | solution.py:152
  94.3 6.0 %collective-permute-done.18.refs_2_ = bf16[192,1664]{1,0:T(8,128)(2,1)S(1)} collective-permute-done((bf16[192,1664]{1,0:T(8,128)(2,1)S(1)}, bf16[192,1664]{1,0:T(8,128)(2,1)S(1)}, u32[]{:S(2)}, u32[]{:S(2)}) %collective-permute-start.18) | collective-permute-done | bytes 639008 | tf_op jit(solution)/shard_map/ppermute | solution.py:54
  103.5 8.2 %collective-permute-done.5.refs_4_ = bf16[160,1664]{1,0:T(8,128)(2,1)S(1)} collective-permute-done((bf16[160,1664]{1,0:T(8,128)(2,1)S(1)}, bf16[160,1664]{1,0:T(8,128)(2,1)S(1)}, u32[]{:S(2)}, u32[]{:S(2)}) %collective-permute-start.5) | collective-permute-done | bytes 532512 | tf_op jit(solution)/shard_map/ppermute | solution.py:54
  113.8 8.5 %shard_map.115 = (bf16[3200,384]{1,0:T(8,128)(2,1)S(1)}, bf16[3200,384]{1,0:T(8,128)(2,1)S(1)}, f32[8,128]{1,0:T(8,128)S(1)}, f32[768,1664]{1,0:T(8,128)S(1)}, b...) custom-call(s32[3]{0:T(128)S(1)} %pad_add_fusion.place.refs_0_, ...), custom_call_target="tpu_custom_call", output_to_operand_aliasing={{0}: (7, {}), {1}: (8, {}), {2}: (9, {}), {3}: (10, {})} | custom-call | tf_op jit(solution)/shard_map/pallas_call | solution.py:152
  122.2 3.2 %collective-permute-done.20.refs_2_ = bf16[192,1664]{1,0:T(8,128)(2,1)S(1)} collective-permute-done((bf16[192,1664]{1,0:T(8,128)(2,1)S(1)}, bf16[192,1664]{1,0:T(8,128)(2,1)S(1)}, u32[]{:S(2)}, u32[]{:S(2)}) %collective-permute-start.20) | collective-permute-done | bytes 639008 | tf_op jit(solution)/shard_map/ppermute | solution.py:54
  128.9 8.7 %collective-permute-done.23.refs_2_ = bf16[192,1664]{1,0:T(8,128)(2,1)S(1)} collective-permute-done((bf16[192,1664]{1,0:T(8,128)(2,1)S(1)}, bf16[192,1664]{1,0:T(8,128)(2,1)S(1)}, u32[]{:S(2)}, u32[]{:S(2)}) %collective-permute-start.23) | collective-permute-done | bytes 639008 | tf_op jit(solution)/shard_map/ppermute | solution.py:54
  148.1 6.7 %shard_map.119 = (bf16[3200,384]{1,0:T(8,128)(2,1)S(1)}, bf16[3200,384]{1,0:T(8,128)(2,1)S(1)}, f32[8,128]{1,0:T(8,128)S(1)}, f32[768,1664]{1,0:T(8,128)S(1)}, b...) custom-call(s32[3]{0:T(128)S(1)} %pad_add_fusion.place.refs_0_, ...), custom_call_target="tpu_custom_call", output_to_operand_aliasing={{0}: (6, {}), {1}: (7, {}), {2}: (8, {}), {3}: (9, {})} | custom-call | tf_op jit(solution)/shard_map/pallas_call | solution.py:152
  154.8 4.4 %shard_map.120 = (bf16[3200,384]{1,0:T(8,128)(2,1)S(1)}, bf16[3200,384]{1,0:T(8,128)(2,1)S(1)}, f32[8,128]{1,0:T(8,128)S(1)}, f32[768,1664]{1,0:T(8,128)S(1)}, bf16[160,1664]{1,0:T(8,128)(2,1)S(1)}) custom-call(s32[3]{0:T(128)S(1)} %pad_add_fusion.place.refs_0_, ...), custom_call_target="tpu_custom_call", output_to_operand_aliasing={{0}: (5, {}), {1}: (6, {}), {2}: (7, {}), {3}: (8, {})} | custom-call | tf_op jit(solution)/shard_map/pallas_call | solution.py:152
  162.9 5.1 %shard_map.121 = (bf16[3200,384]{1,0:T(8,128)(2,1)S(1)}, bf16[3200,384]{1,0:T(8,128)(2,1)S(1)}, f32[8,128]{1,0:T(8,128)S(1)}, f32[768,1664]{1,0:T(8,128)S(1)}, b...) custom-call(s32[3]{0:T(128)S(1)} %pad_add_fusion.place.refs_0_, ...), custom_call_target="tpu_custom_call", output_to_operand_aliasing={{0}: (6, {}), {1}: (7, {}), {2}: (8, {}), {3}: (9, {})} | custom-call | tf_op jit(solution)/shard_map/pallas_call | solution.py:152
  172.5 8.7 %collective-permute-done.3.refs_4_ = bf16[96,1664]{1,0:T(8,128)(2,1)S(1)} collective-permute-done((bf16[96,1664]{1,0:T(8,128)(2,1)S(1)}, bf16[96,1664]{1,0:T(8,128)(2,1)S(1)}, u32[]{:S(2)}, u32[]{:S(2)}) %collective-permute-start.3) | collective-permute-done | bytes 319520 | tf_op jit(solution)/shard_map/ppermute | solution.py:54
  181.7 3.4 %shard_map.125 = (bf16[3200,384]{1,0:T(8,128)(2,1)S(1)}, bf16[3200,384]{1,0:T(8,128)(2,1)S(1)}, f32[8,128]{1,0:T(8,128)S(1)}, f32[768,1664]{1,0:T(8,128)S(1)}, bf16[96,1664]{1,0:T(8,128)(2,1)}) custom-call(s32[3]{0:T(128)S(1)} %pad_add_fusion.place.refs_0_, ...), custom_call_target="tpu_custom_call", output_to_operand_aliasing={{0}: (5, {}), {1}: (6, {}), {2}: (7, {}), {3}: (8, {})} | custom-call | tf_op jit(solution)/shard_map/pallas_call | solution.py:152
  191.8 5.4 %shard_map.128 = (f32[8,128]{1,0:T(8,128)S(1)}, f32[8,1600]{1,0:T(8,128)S(1)}) custom-call(f32[768,1664]{1,0:T(8,128)S(1)} %get-tuple-element.243.acc, bf16[768,1600]{1,0:T(8,128)(2,1)S(1)} %get-tuple-element.248.plain, f32[8,128]{1,0:T(8,128)S(1)} %get-tuple-element.254.token), custom_call_target="tpu_custom_call", output_to_operand_aliasing={{0}: (2, {})} | custom-call | tf_op jit(solution)/shard_map/pallas_call | solution.py:152
  237.2 7.1 %collective-permute-done.47.refs_2_ = bf16[80,1664]{1,0:T(8,128)(2,1)} collective-permute-done((bf16[80,1664]{1,0:T(8,128)(2,1)}, bf16[80,1664]{1,0:T(8,128)(2,1)}, u32[]{:S(2)}, u32[]{:S(2)}) %collective-permute-start.47) | collective-permute-done | bytes 266272 | tf_op jit(solution)/shard_map/ppermute | solution.py:518
  258.5 6.6 %collective-permute-done.49.refs_2_ = bf16[48,1664]{1,0:T(8,128)(2,1)S(1)} collective-permute-done((bf16[48,1664]{1,0:T(8,128)(2,1)S(1)}, bf16[48,1664]{1,0:T(8,128)(2,1)S(1)}, u32[]{:S(2)}, u32[]{:S(2)}) %collective-permute-start.49) | collective-permute-done | bytes 159776 | tf_op jit(solution)/shard_map/ppermute | solution.py:518
  266.6 4.1 %shard_map.146 = (f32[8,128]{1,0:T(8,128)S(1)}, bf16[384,6400]{1,0:T(8,128)(2,1)}) custom-call(s32[3]{0:T(128)S(1)} %pad_add_fusion.place.refs_0_, bf16[3200,384]{1,0:T(8,128)(2,1)S(1)} %get-tuple-element.242.own, bf16[3200,384]{1,0:T(8,128)(2,1)S(1)} %collective-permute-done.48.peer, ...), custom_call_target="tpu_custom_call", output_to_operand_aliasing={{0}: (3, {})} | custom-call | tf_op jit(solution)/shard_map/pallas_call | solution.py:152
  (218 shorter events, 136.3 us)
Async XLA Ops:
  7.9 26.2 %collective-permute-start.13 = (bf16[192,1664]{1,0:T(8,128)(2,1)}, bf16[192,1664]{1,0:T(8,128)(2,1)}, u32[]{:S(2)}, u32[]{:S(2)}) collective-permute-start(bf16[192,1664]{1,0:T(8,128)(2,1)} %get-tuple-element.164.refs_4_), channel_id=1, source_target_pairs={{0,16},{4,20},{8,24},{12,28},{16,0},{20,4},{24,8},{28,12},{1,17},{... | collective-permute-start | bytes 1916936 | tf_op jit(solution)/shard_map/ppermute | solution.py:54
  11.0 25.8 %collective-permute-start.12 = (bf16[192,1664]{1,0:T(8,128)(2,1)}, bf16[192,1664]{1,0:T(8,128)(2,1)}, u32[]{:S(2)}, u32[]{:S(2)}) collective-permute-start(bf16[192,1664]{1,0:T(8,128)(2,1)} %get-tuple-element.164.refs_4_), channel_id=1, source_target_pairs={{0,8},{4,12},{8,0},{12,4},{16,24},{20,28},{24,16},{28,20},{1,9},{5... | collective-permute-start | bytes 1916936 | tf_op jit(solution)/shard_map/ppermute | solution.py:54
  12.6 32.7 %collective-permute-start.11 = (bf16[192,1664]{1,0:T(8,128)(2,1)}, bf16[192,1664]{1,0:T(8,128)(2,1)S(1)}, u32[]{:S(2)}, u32[]{:S(2)}) collective-permute-start(bf16[192,1664]{1,0:T(8,128)(2,1)} %copy-done.14), channel_id=1, source_target_pairs={{0,8},{4,12},{8,0},{12,4},{16,24},{20,28},{24,16},{28,20},{1,9},{5... | collective-permute-start | bytes 1916936 | tf_op jit(solution)/shard_map/ppermute | solution.py:54
  13.8 32.9 %collective-permute-start.17 = (bf16[192,1664]{1,0:T(8,128)(2,1)}, bf16[192,1664]{1,0:T(8,128)(2,1)S(1)}, u32[]{:S(2)}, u32[]{:S(2)}) collective-permute-start(bf16[192,1664]{1,0:T(8,128)(2,1)} %copy-done.14), channel_id=1, source_target_pairs={{0,16},{4,20},{8,24},{12,28},{16,0},{20,4},{24,8},{28,12},{1,17},{... | collective-permute-start | bytes 1916936 | tf_op jit(solution)/shard_map/ppermute | solution.py:54
  35.8 26.1 %collective-permute-start.8 = (bf16[160,1664]{1,0:T(8,128)(2,1)S(1)}, bf16[160,1664]{1,0:T(8,128)(2,1)S(1)}, u32[]{:S(2)}, u32[]{:S(2)}) collective-permute-start(bf16[160,1664]{1,0:T(8,128)(2,1)S(1)} %copy-done.19), channel_id=1, source_target_pairs={{0,16},{4,20},{8,24},{12,28},{16,0},{20,4},{24,8},{28,12},{1,17},{... | collective-permute-start | bytes 1597448 | tf_op jit(solution)/shard_map/ppermute | solution.py:54
  59.9 31.0 %collective-permute-start.19 = (bf16[192,1664]{1,0:T(8,128)(2,1)S(1)}, bf16[192,1664]{1,0:T(8,128)(2,1)S(1)}, u32[]{:S(2)}, u32[]{:S(2)}) collective-permute-start(bf16[192,1664]{1,0:T(8,128)(2,1)S(1)} %get-tuple-element.202), channel_id=1, source_target_pairs={{0,16},{4,20},{8,24},{12,28},{16,0},{20,4},{24,8},{28,12},{1,17},{... | collective-permute-start | bytes 1916936 | tf_op jit(solution)/shard_map/ppermute | solution.py:54
  61.9 24.7 %collective-permute-start.9 = (bf16[160,1664]{1,0:T(8,128)(2,1)S(1)}, bf16[160,1664]{1,0:T(8,128)(2,1)S(1)}, u32[]{:S(2)}, u32[]{:S(2)}) collective-permute-start(bf16[160,1664]{1,0:T(8,128)(2,1)S(1)} %collective-permute-done.8.refs_5_), channel_id=1, source_target_pairs={{0,8},{4,12},{8,0},{12,4},{16,24},{20,28},{24,16},{28,20},{1,9},{5... | collective-permute-start | bytes 1597448 | tf_op jit(solution)/shard_map/ppermute | solution.py:54
  69.5 30.8 %collective-permute-start.18 = (bf16[192,1664]{1,0:T(8,128)(2,1)S(1)}, bf16[192,1664]{1,0:T(8,128)(2,1)S(1)}, u32[]{:S(2)}, u32[]{:S(2)}) collective-permute-start(bf16[192,1664]{1,0:T(8,128)(2,1)S(1)} %get-tuple-element.200), channel_id=1, source_target_pairs={{0,8},{4,12},{8,0},{12,4},{16,24},{20,28},{24,16},{28,20},{1,9},{5... | collective-permute-start | bytes 1916936 | tf_op jit(solution)/shard_map/ppermute | solution.py:54
  71.6 41.9 %collective-permute-start.21 = (bf16[192,1664]{1,0:T(8,128)(2,1)S(1)}, bf16[192,1664]{1,0:T(8,128)(2,1)S(1)}, u32[]{:S(2)}, u32[]{:S(2)}) collective-permute-start(bf16[192,1664]{1,0:T(8,128)(2,1)S(1)} %get-tuple-element.211), channel_id=1, source_target_pairs={{0,16},{4,20},{8,24},{12,28},{16,0},{20,4},{24,8},{28,12},{1,17},{... | collective-permute-start | bytes 1916936 | tf_op jit(solution)/shard_map/ppermute | solution.py:54
  75.2 36.5 %collective-permute-start.5 = (bf16[160,1664]{1,0:T(8,128)(2,1)S(1)}, bf16[160,1664]{1,0:T(8,128)(2,1)S(1)}, u32[]{:S(2)}, u32[]{:S(2)}) collective-permute-start(bf16[160,1664]{1,0:T(8,128)(2,1)S(1)} %copy-done.17), channel_id=1, source_target_pairs={{0,8},{4,12},{8,0},{12,4},{16,24},{20,28},{24,16},{28,20},{1,9},{5... | collective-permute-start | bytes 1597448 | tf_op jit(solution)/shard_map/ppermute | solution.py:54
  92.2 33.2 %collective-permute-start.20 = (bf16[192,1664]{1,0:T(8,128)(2,1)S(1)}, bf16[192,1664]{1,0:T(8,128)(2,1)S(1)}, u32[]{:S(2)}, u32[]{:S(2)}) collective-permute-start(bf16[192,1664]{1,0:T(8,128)(2,1)S(1)} %get-tuple-element.210), channel_id=1, source_target_pairs={{0,8},{4,12},{8,0},{12,4},{16,24},{20,28},{24,16},{28,20},{1,9},{5... | collective-permute-start | bytes 1916936 | tf_op jit(solution)/shard_map/ppermute | solution.py:54
  94.0 43.6 %collective-permute-start.23 = (bf16[192,1664]{1,0:T(8,128)(2,1)S(1)}, bf16[192,1664]{1,0:T(8,128)(2,1)S(1)}, u32[]{:S(2)}, u32[]{:S(2)}) collective-permute-start(bf16[192,1664]{1,0:T(8,128)(2,1)S(1)} %get-tuple-element.216), channel_id=1, source_target_pairs={{0,8},{4,12},{8,0},{12,4},{16,24},{20,28},{24,16},{28,20},{1,9},{5... | collective-permute-start | bytes 1916936 | tf_op jit(solution)/shard_map/ppermute | solution.py:54
  101.7 37.6 %collective-permute-start.24 = (bf16[192,1664]{1,0:T(8,128)(2,1)S(1)}, bf16[192,1664]{1,0:T(8,128)(2,1)S(1)}, u32[]{:S(2)}, u32[]{:S(2)}) collective-permute-start(bf16[192,1664]{1,0:T(8,128)(2,1)S(1)} %get-tuple-element.217), channel_id=1, source_target_pairs={{0,16},{4,20},{8,24},{12,28},{16,0},{20,4},{24,8},{28,12},{1,17},{... | collective-permute-start | bytes 1916936 | tf_op jit(solution)/shard_map/ppermute | solution.py:54
  111.7 32.1 %collective-permute-start.7 = (bf16[160,1664]{1,0:T(8,128)(2,1)S(1)}, bf16[160,1664]{1,0:T(8,128)(2,1)S(1)}, u32[]{:S(2)}, u32[]{:S(2)}) collective-permute-start(bf16[160,1664]{1,0:T(8,128)(2,1)S(1)} %copy-done.17), channel_id=1, source_target_pairs={{0,16},{4,20},{8,24},{12,28},{16,0},{20,4},{24,8},{28,12},{1,17},{... | collective-permute-start | bytes 1597448 | tf_op jit(solution)/shard_map/ppermute | solution.py:54
  113.5 33.0 %collective-permute-start.6 = (bf16[160,1664]{1,0:T(8,128)(2,1)S(1)}, bf16[160,1664]{1,0:T(8,128)(2,1)S(1)}, u32[]{:S(2)}, u32[]{:S(2)}) collective-permute-start(bf16[160,1664]{1,0:T(8,128)(2,1)S(1)} %collective-permute-done.5.refs_4_), channel_id=1, source_target_pairs={{0,16},{4,20},{8,24},{12,28},{16,0},{20,4},{24,8},{28,12},{1,17},{... | collective-permute-start | bytes 1597448 | tf_op jit(solution)/shard_map/ppermute | solution.py:54
  137.6 21.6 %collective-permute-start.2 = (bf16[96,1664]{1,0:T(8,128)(2,1)S(1)}, bf16[96,1664]{1,0:T(8,128)(2,1)S(1)}, u32[]{:S(2)}, u32[]{:S(2)}) collective-permute-start(bf16[96,1664]{1,0:T(8,128)(2,1)S(1)} %get-tuple-element.160.refs_6_), channel_id=1, source_target_pairs={{0,16},{4,20},{8,24},{12,28},{16,0},{20,4},{24,8},{28,12},{1,17},{... | collective-permute-start | bytes 958472 | tf_op jit(solution)/shard_map/ppermute | solution.py:54
  139.2 31.3 %collective-permute-start.25 = (bf16[160,1664]{1,0:T(8,128)(2,1)S(1)}, bf16[160,1664]{1,0:T(8,128)(2,1)S(1)}, u32[]{:S(2)}, u32[]{:S(2)}) collective-permute-start(bf16[160,1664]{1,0:T(8,128)(2,1)S(1)} %get-tuple-element.233), channel_id=1, source_target_pairs={{0,16},{4,20},{8,24},{12,28},{16,0},{20,4},{24,8},{28,12},{1,17},{... | collective-permute-start | bytes 1597448 | tf_op jit(solution)/shard_map/ppermute | solution.py:54
  146.5 22.5 %collective-permute-start.26 = (bf16[96,1664]{1,0:T(8,128)(2,1)S(1)}, bf16[96,1664]{1,0:T(8,128)(2,1)S(1)}, u32[]{:S(2)}, u32[]{:S(2)}) collective-permute-start(bf16[96,1664]{1,0:T(8,128)(2,1)S(1)} %get-tuple-element.235), channel_id=1, source_target_pairs={{0,1},{1,0},{2,3},{3,2},{4,5},{5,4},{6,7},{7,6},{8,9},{9,8},{10,11... | collective-permute-start | bytes 958472 | tf_op jit(solution)/shard_map/ppermute | solution.py:518
  159.3 25.9 %collective-permute-start.31 = (bf16[160,1664]{1,0:T(8,128)(2,1)S(1)}, bf16[160,1664]{1,0:T(8,128)(2,1)S(1)}, u32[]{:S(2)}, u32[]{:S(2)}) collective-permute-start(bf16[160,1664]{1,0:T(8,128)(2,1)S(1)} %get-tuple-element.251), channel_id=1, source_target_pairs={{0,8},{4,12},{8,0},{12,4},{16,24},{20,28},{24,16},{28,20},{1,9},{5... | collective-permute-start | bytes 1597448 | tf_op jit(solution)/shard_map/ppermute | solution.py:54
  159.9 29.1 %collective-permute-start.29 = (bf16[160,1664]{1,0:T(8,128)(2,1)S(1)}, bf16[160,1664]{1,0:T(8,128)(2,1)S(1)}, u32[]{:S(2)}, u32[]{:S(2)}) collective-permute-start(bf16[160,1664]{1,0:T(8,128)(2,1)S(1)} %get-tuple-element.247), channel_id=1, source_target_pairs={{0,16},{4,20},{8,24},{12,28},{16,0},{20,4},{24,8},{28,12},{1,17},{... | collective-permute-start | bytes 1597448 | tf_op jit(solution)/shard_map/ppermute | solution.py:54
  171.4 25.8 %collective-permute-start.28 = (bf16[160,1664]{1,0:T(8,128)(2,1)S(1)}, bf16[160,1664]{1,0:T(8,128)(2,1)S(1)}, u32[]{:S(2)}, u32[]{:S(2)}) collective-permute-start(bf16[160,1664]{1,0:T(8,128)(2,1)S(1)} %get-tuple-element.246), channel_id=1, source_target_pairs={{0,8},{4,12},{8,0},{12,4},{16,24},{20,28},{24,16},{28,20},{1,9},{5... | collective-permute-start | bytes 1597448 | tf_op jit(solution)/shard_map/ppermute | solution.py:54
  181.2 32.0 %collective-permute-start.39 = (bf16[160,1664]{1,0:T(8,128)(2,1)}, bf16[160,1664]{1,0:T(8,128)(2,1)S(1)}, u32[]{:S(2)}, u32[]{:S(2)}) collective-permute-start(bf16[160,1664]{1,0:T(8,128)(2,1)} %get-tuple-element.268), channel_id=1, source_target_pairs={{0,8},{4,12},{8,0},{12,4},{16,24},{20,28},{24,16},{28,20},{1,9},{5... | collective-permute-start | bytes 1597448 | tf_op jit(solution)/shard_map/ppermute | solution.py:54
  187.4 25.8 %collective-permute-start.40 = (bf16[160,1664]{1,0:T(8,128)(2,1)}, bf16[160,1664]{1,0:T(8,128)(2,1)}, u32[]{:S(2)}, u32[]{:S(2)}) collective-permute-start(bf16[160,1664]{1,0:T(8,128)(2,1)} %get-tuple-element.269), channel_id=1, source_target_pairs={{0,16},{4,20},{8,24},{12,28},{16,0},{20,4},{24,8},{28,12},{1,17},{... | collective-permute-start | bytes 1597448 | tf_op jit(solution)/shard_map/ppermute | solution.py:54
  202.6 22.0 %collective-permute-start.38 = (bf16[96,1664]{1,0:T(8,128)(2,1)S(1)}, bf16[96,1664]{1,0:T(8,128)(2,1)S(1)}, u32[]{:S(2)}, u32[]{:S(2)}) collective-permute-start(bf16[96,1664]{1,0:T(8,128)(2,1)S(1)} %get-tuple-element.266.mine), channel_id=1, source_target_pairs={{0,1},{1,0},{2,3},{3,2},{4,5},{5,4},{6,7},{7,6},{8,9},{9,8},{10,11... | collective-permute-start | bytes 958472 | tf_op jit(solution)/shard_map/ppermute | solution.py:518
  (60 other events, 741.3 us)
